TPU v7x, 128 devices: a whole 4x4x4 slice. The times are simulated.
128 devices in a mesh: grp: 2 (over y_lo), dev: 64 (over z, x, y_hi, core).
Axes of the slice: x: 4, y: 4 (y_hi: 2, y_lo: 2; y = y_hi * 2 + y_lo), z: 4, core: 2. Of those that a mesh axis runs over, the one named last changes fastest.
Arguments:
- images: bfloat16 [114688, 1152], P(('grp', 'dev')), may hold values from -6 to 6
- texts: bfloat16 [114688, 1152], P(('grp', 'dev')), may hold values from -6 to 6
- image_partner: int32 [114688], P(('grp', 'dev')), may hold values from 0 to 114687, as said below
- text_partner: int32 [114688], P(('grp', 'dev')), may hold values from 0 to 114687, as said below
Outputs:
- grad_images: float32 [114688, 1152], P(('grp', 'dev'))
- grad_texts: float32 [114688, 1152], P(('grp', 'dev'))
Inputs may be any that keep to these rules, and one draw needn't show every extreme that they name: image_partner is a permutation of the text indices that maps each block of 896 rows onto itself. text_partner is the inverse permutation of image_partner: text_partner[image_partner[i]] == i.
All inputs are finite; a program needn't handle non-finite values.
Results may differ from a plain program's by a relative error of at most 0.0017.
Values may be sent and summed in bfloat16 or wider, within the bound.
No kernel may reach another device: no remote copies, remote signals or barrier semaphores. Data moves between devices by JAX's collectives and lax.ppermute only.
A program may use at most 128 MiB of HBM per device.

v0:
```python
import jax
import jax.numpy as jnp
from jax import lax
from jax.sharding import PartitionSpec as P

ROUNDS = 2


def from_behind(block, axis, distance):
    devices = range(lax.axis_size(axis))
    route = [((i - distance) % len(devices), i) for i in devices]
    return lax.ppermute(block, axis, route)


def own_weights(left, right, signs, temp):
    logits = (
        temp
        * lax.dot_general(left, right, (((1,), (1,)), ((), ())), preferred_element_type=jnp.float32)
        - 2.0
    )
    return (-signs * jax.nn.sigmoid(-signs * logits) * temp).astype(jnp.bfloat16)


def cross_weights(left, right, temp):
    logits = (
        temp
        * lax.dot_general(left, right, (((1,), (1,)), ((), ())), preferred_element_type=jnp.float32)
        - 2.0
    )
    return (jax.nn.sigmoid(logits) * temp).astype(jnp.bfloat16)


def shards(images, texts, image_partner, text_partner):
    width = images.shape[1]
    local_rows = images.shape[0]
    temp = 2.0 * width ** (-0.5)
    contract_rows = (((0,), (0,)), ((), ()))
    start = lax.axis_index(("grp", "dev")) * local_rows
    row_ids = start + jnp.arange(local_rows, dtype=jnp.int32)
    sign_img = jnp.where(image_partner[:, None] == row_ids[None, :], 1.0, -1.0).astype(jnp.float32)
    sign_txt = jnp.where(text_partner[None, :] == row_ids[:, None], 1.0, -1.0).astype(jnp.float32)
    weight_img = own_weights(images, texts, sign_img, temp)
    weight_txt = own_weights(images, texts, sign_txt, temp)
    grad_images = jnp.dot(weight_img, texts, preferred_element_type=jnp.float32)
    grad_texts = lax.dot_general(
        weight_txt, images, contract_rows, preferred_element_type=jnp.float32
    )
    for rounds_ahead in range(1, ROUNDS + 1):
        got_img, got_txt = from_behind((images, texts), ("grp", "dev"), rounds_ahead)
        weight_a = cross_weights(images, got_txt, temp)
        grad_images = grad_images + jnp.dot(weight_a, got_txt, preferred_element_type=jnp.float32)
        back_txt = lax.dot_general(
            weight_a, images, contract_rows, preferred_element_type=jnp.float32
        )
        weight_b = cross_weights(got_img, texts, temp)
        grad_texts = grad_texts + lax.dot_general(
            weight_b, got_img, contract_rows, preferred_element_type=jnp.float32
        )
        back_img = jnp.dot(weight_b, texts, preferred_element_type=jnp.float32)
        ret_img, ret_txt = from_behind((back_img, back_txt), ("grp", "dev"), -rounds_ahead)
        grad_images = grad_images + ret_img
        grad_texts = grad_texts + ret_txt
    return (grad_images, grad_texts)


def solution(mesh):
    return jax.shard_map(
        shards,
        mesh=mesh,
        in_specs=(
            P(("grp", "dev"), None),
            P(("grp", "dev"), None),
            P(("grp", "dev")),
            P(("grp", "dev")),
        ),
        out_specs=(P(("grp", "dev"), None), P(("grp", "dev"), None)),
        check_vma=False,
    )
```

profile of v0, /device:TPU:55, one launch (start us, length us, event | category | flops | bytes accessed | tf_op | source)
XLA Modules:
  0.0 492.9 jit_solution(8635512534497089869)
XLA Ops:
  0.6 0.0 copy-start.6
  0.6 1.4 collective-permute-start.4
  2.0 3.8 collective-permute-start.1
  5.8 1.0 collective-permute-start.3
  6.8 0.3 collective-permute-start
  7.1 41.1 %collective-permute-done.4 = bf16[896,1152]{1,0:T(8,128)(2,1)S(1)} collective-permute-done((bf16[896,1152]{1,0:T(8,128)(2,1)}, bf16[896,1152]{1,0:T(8,128)(2,1)S(1)}, u32[]{:S(2)}, u32[]{:S(2)}) %collective-permute-start.4) | collective-permute-done | bytes 2064416 | tf_op jit(solution)/shard_map/ppermute | solution.py:12
  48.2 5.0 %multiply_convert_fusion.1 = bf16[896,896]{1,0:T(8,128)(2,1)S(1)} fusion(bf16[896,1152]{1,0:T(8,128)(2,1)S(1)} %collective-permute-done.4, bf16[896,1152]{1,0:T(8,128)(2,1)} %param.5), kind=kOutput, calls=%fused_computation.9 | convolution fusion | flops 1855307776 | bytes 5734400 | tf_op jit(solution)/shard_map/dot_general | solution.py:27
  53.3 4.5 fusion.31
  57.8 1.0 collective-permute-start.5
  58.8 31.5 %collective-permute-done.1 = bf16[896,1152]{1,0:T(8,128)(2,1)S(1)} collective-permute-done((bf16[896,1152]{1,0:T(8,128)(2,1)}, bf16[896,1152]{1,0:T(8,128)(2,1)S(1)}, u32[]{:S(2)}, u32[]{:S(2)}) %collective-permute-start.1) | collective-permute-done | bytes 2064416 | tf_op jit(solution)/shard_map/ppermute | solution.py:12
  90.2 2.7 multiply_convert_fusion.3
  93.0 0.0 copy-start.7
  93.0 4.5 fusion.29
  97.5 135.8 %collective-permute-start.2 = (f32[896,1152]{1,0:T(8,128)}, f32[896,1152]{1,0:T(8,128)}, u32[]{:S(2)}, u32[]{:S(2)}) collective-permute-start(f32[896,1152]{1,0:T(8,128)} %fusion.29), channel_id=1, source_target_pairs={{1,0},{2,1},{3,2},{4,3},{5,4},{6,5},{7,6},{8,7},{9,8},{10,9},{11,1... | collective-permute-start | bytes 12386312 | tf_op jit(solution)/shard_map/ppermute | solution.py:12
  233.3 147.6 %collective-permute-done.3 = bf16[896,1152]{1,0:T(8,128)(2,1)S(1)} collective-permute-done((bf16[896,1152]{1,0:T(8,128)(2,1)}, bf16[896,1152]{1,0:T(8,128)(2,1)S(1)}, u32[]{:S(2)}, u32[]{:S(2)}) %collective-permute-start.3) | collective-permute-done | bytes 2064416 | tf_op jit(solution)/shard_map/ppermute | solution.py:12
  380.9 2.7 multiply_convert_fusion.2
  383.6 4.5 fusion.34
  388.1 0.0 collective-permute-start.7
  388.1 0.0 collective-permute-done
  388.1 2.7 multiply_convert_fusion.4
  390.8 4.5 fusion.32
  395.3 15.7 %collective-permute-start.6 = (f32[896,1152]{1,0:T(8,128)}, f32[896,1152]{1,0:T(8,128)}, u32[]{:S(2)}, u32[]{:S(2)}) collective-permute-start(f32[896,1152]{1,0:T(8,128)} %fusion.32), channel_id=1, source_target_pairs={{1,0},{2,1},{3,2},{4,3},{5,4},{6,5},{7,6},{8,7},{9,8},{10,9},{11,1... | collective-permute-start | bytes 12386312 | tf_op jit(solution)/shard_map/ppermute | solution.py:12
  411.1 4.2 fusion.28
  415.3 6.0 %fusion.6 = f32[896,1152]{1,0:T(8,128)S(1)} fusion(bf16[896,1152]{1,0:T(8,128)(2,1)} %param.5, f32[896,896]{1,0:T(8,128)} %fusion.28, s32[896]{0:T(1024)S(1)} %iota_add_fusion, s32[896]{0:T(1024)S(1)} %copy-done.13), kind=kOutput, calls=%fused_computation.15 | convolution fusion | flops 1859321856 | bytes 9411584 | tf_op jit(solution)/shard_map/dot_general | solution.py:44
  421.4 3.4 fusion.7
  424.9 2.5 fusion.30
  427.4 2.8 fusion.33
  430.2 0.0 collective-permute-done.5
  430.3 8.4 %fusion.5 = f32[896,1152]{1,0:T(8,128)} fusion(f32[896,1152]{1,0:T(8,128)} %collective-permute-done.5, f32[896,1152]{1,0:T(8,128)S(1)} %fusion.30, f32[896,1152]{1,0:T(8,128)} %collective-permute-done.2, f32[896,1152]{1,0:T(8,128)S(1)} %fusion.6, bf16[896,896]{1,0:T(8,128)(2,1)S(1)} %copy-done.5, bf16[896,1152]{1,0:T(8,128)(2,1)S(1)} %copy-done.1), kind=kOutput, calls=%fused_computation.7 | convolution fusion | flops 1853816832 | bytes 24313856 | tf_op jit(solution)/shard_map/dot_general | solution.py:51
  438.7 37.1 %collective-permute-done.7 = f32[896,1152]{1,0:T(8,128)} collective-permute-done((f32[896,1152]{1,0:T(8,128)}, f32[896,1152]{1,0:T(8,128)}, u32[]{:S(2)}, u32[]{:S(2)}) %collective-permute-start.7) | collective-permute-done | bytes 4128800 | tf_op jit(solution)/shard_map/ppermute | solution.py:12
  475.7 8.1 %collective-permute-done.6 = f32[896,1152]{1,0:T(8,128)} collective-permute-done((f32[896,1152]{1,0:T(8,128)}, f32[896,1152]{1,0:T(8,128)}, u32[]{:S(2)}, u32[]{:S(2)}) %collective-permute-start.6) | collective-permute-done | bytes 4128800 | tf_op jit(solution)/shard_map/ppermute | solution.py:12
  483.8 8.9 %fusion.2 = f32[896,1152]{1,0:T(8,128)} fusion(f32[896,1152]{1,0:T(8,128)} %collective-permute-done.7, f32[896,1152]{1,0:T(8,128)S(1)} %fusion.33, f32[896,1152]{1,0:T(8,128)} %collective-permute-done.6, f32[896,1152]{1,0:T(8,128)S(1)} %fusion.7, bf16[896,896]{1,0:T(8,128)(2,1)S(1)} %copy-done.3, bf16[896,1152]{1,0:T(8,128)(2,1)S(1)} %collective-permute-done.1), kind=kOutput, calls=%fused_computation.3 | convolution fusion | flops 1853816832 | bytes 24313856 | tf_op jit(solution)/shard_map/dot_general | solution.py:56
  (40 shorter events, 0.1 us)
Async XLA Ops:
  0.6 52.7 %copy-start.6 = (bf16[896,1152]{1,0:T(8,128)(2,1)S(1)}, bf16[896,1152]{1,0:T(8,128)(2,1)}, u32[]{:S(2)}) copy-start(bf16[896,1152]{1,0:T(8,128)(2,1)} %param.5) | copy-start | bytes 6193156
  0.6 47.6 %collective-permute-start.4 = (bf16[896,1152]{1,0:T(8,128)(2,1)}, bf16[896,1152]{1,0:T(8,128)(2,1)S(1)}, u32[]{:S(2)}, u32[]{:S(2)}) collective-permute-start(bf16[896,1152]{1,0:T(8,128)(2,1)} %param.4), channel_id=1, source_target_pairs={{126,0},{127,1},{0,2},{1,3},{2,4},{3,5},{4,6},{5,7},{6,8},{7,9},{8... | collective-permute-start | bytes 6193160 | tf_op jit(solution)/shard_map/ppermute | solution.py:12
  2.0 88.2 %collective-permute-start.1 = (bf16[896,1152]{1,0:T(8,128)(2,1)}, bf16[896,1152]{1,0:T(8,128)(2,1)S(1)}, u32[]{:S(2)}, u32[]{:S(2)}) collective-permute-start(bf16[896,1152]{1,0:T(8,128)(2,1)} %param.4), channel_id=1, source_target_pairs={{127,0},{0,1},{1,2},{2,3},{3,4},{4,5},{5,6},{6,7},{7,8},{8,9},{9,1... | collective-permute-start | bytes 6193160 | tf_op jit(solution)/shard_map/ppermute | solution.py:12
  5.8 375.1 %collective-permute-start.3 = (bf16[896,1152]{1,0:T(8,128)(2,1)}, bf16[896,1152]{1,0:T(8,128)(2,1)S(1)}, u32[]{:S(2)}, u32[]{:S(2)}) collective-permute-start(bf16[896,1152]{1,0:T(8,128)(2,1)} %param.5), channel_id=1, source_target_pairs={{126,0},{127,1},{0,2},{1,3},{2,4},{3,5},{4,6},{5,7},{6,8},{7,9},{8... | collective-permute-start | bytes 6193160 | tf_op jit(solution)/shard_map/ppermute | solution.py:12
  6.8 381.3 %collective-permute-start = (bf16[896,1152]{1,0:T(8,128)(2,1)}, bf16[896,1152]{1,0:T(8,128)(2,1)S(1)}, u32[]{:S(2)}, u32[]{:S(2)}) collective-permute-start(bf16[896,1152]{1,0:T(8,128)(2,1)} %param.5), channel_id=1, source_target_pairs={{127,0},{0,1},{1,2},{2,3},{3,4},{4,5},{5,6},{6,7},{7,8},{8,9},{9,1... | collective-permute-start | bytes 6193160 | tf_op jit(solution)/shard_map/ppermute | solution.py:12
  48.2 5.1 %copy-start.9 = (bf16[896,1152]{1,0:T(8,128)(2,1)}, bf16[896,1152]{1,0:T(8,128)(2,1)S(1)}, u32[]{:S(2)}) copy-start(bf16[896,1152]{1,0:T(8,128)(2,1)S(1)} %collective-permute-done.4) | copy-start | bytes 6193156
  53.3 4.5 copy-start.16
  57.8 372.4 %collective-permute-start.5 = (f32[896,1152]{1,0:T(8,128)}, f32[896,1152]{1,0:T(8,128)}, u32[]{:S(2)}, u32[]{:S(2)}) collective-permute-start(f32[896,1152]{1,0:T(8,128)} %fusion.31), channel_id=1, source_target_pairs={{2,0},{3,1},{4,2},{5,3},{6,4},{7,5},{8,6},{9,7},{10,8},{11,9},{12,... | collective-permute-start | bytes 12386312 | tf_op jit(solution)/shard_map/ppermute | solution.py:12
  93.0 4.5 copy-start.2
  93.0 287.9 %copy-start.7 = (bf16[896,1152]{1,0:T(8,128)(2,1)S(1)}, bf16[896,1152]{1,0:T(8,128)(2,1)}, u32[]{:S(2)}) copy-start(bf16[896,1152]{1,0:T(8,128)(2,1)} %param.4) | copy-start | bytes 6193156
  97.5 332.8 %collective-permute-start.2 = (f32[896,1152]{1,0:T(8,128)}, f32[896,1152]{1,0:T(8,128)}, u32[]{:S(2)}, u32[]{:S(2)}) collective-permute-start(f32[896,1152]{1,0:T(8,128)} %fusion.29), channel_id=1, source_target_pairs={{1,0},{2,1},{3,2},{4,3},{5,4},{6,5},{7,6},{8,7},{9,8},{10,9},{11,1... | collective-permute-start | bytes 12386312 | tf_op jit(solution)/shard_map/ppermute | solution.py:12
  380.9 2.7 copy-start.11
  383.6 4.5 copy-start.18
  388.1 87.7 %collective-permute-start.7 = (f32[896,1152]{1,0:T(8,128)}, f32[896,1152]{1,0:T(8,128)}, u32[]{:S(2)}, u32[]{:S(2)}) collective-permute-start(f32[896,1152]{1,0:T(8,128)} %fusion.34), channel_id=1, source_target_pairs={{2,0},{3,1},{4,2},{5,3},{6,4},{7,5},{8,6},{9,7},{10,8},{11,9},{12,... | collective-permute-start | bytes 12386312 | tf_op jit(solution)/shard_map/ppermute | solution.py:12
  388.1 2.7 copy-start
  390.8 4.5 copy-start.4
  395.3 20.0 %copy-start.13 = (s32[896]{0:T(1024)S(1)}, s32[896]{0:T(1024)}, u32[]{:S(2)}) copy-start(s32[896]{0:T(1024)} %param.6) | copy-start | bytes 10756
  395.3 88.5 %collective-permute-start.6 = (f32[896,1152]{1,0:T(8,128)}, f32[896,1152]{1,0:T(8,128)}, u32[]{:S(2)}, u32[]{:S(2)}) collective-permute-start(f32[896,1152]{1,0:T(8,128)} %fusion.32), channel_id=1, source_target_pairs={{1,0},{2,1},{3,2},{4,3},{5,4},{6,5},{7,6},{8,7},{9,8},{10,9},{11,1... | collective-permute-start | bytes 12386312 | tf_op jit(solution)/shard_map/ppermute | solution.py:12
  415.3 6.1 %copy-start.8 = (bf16[896,1152]{1,0:T(8,128)(2,1)S(1)}, bf16[896,1152]{1,0:T(8,128)(2,1)}, u32[]{:S(2)}) copy-start(bf16[896,1152]{1,0:T(8,128)(2,1)} %param.4) | copy-start | bytes 6193156
  415.3 6.1 %copy-start.14 = (s32[896]{0:T(1024)S(1)}, s32[896]{0:T(1024)}, u32[]{:S(2)}) copy-start(s32[896]{0:T(1024)} %param.7) | copy-start | bytes 10756
  415.3 6.1 %copy-start.15 = (f32[896,896]{1,0:T(8,128)S(1)}, f32[896,896]{1,0:T(8,128)}, u32[]{:S(2)}) copy-start(f32[896,896]{1,0:T(8,128)} %fusion.28) | copy-start | bytes 9633796
  421.4 3.4 copy-start.12
  421.4 3.4 copy-start.19
  424.8 2.5 copy-start.10
  424.8 2.5 copy-start.17
  427.4 2.9 copy-start.1
  427.4 2.9 copy-start.5
  430.2 53.6 %copy-start.3 = (bf16[896,896]{1,0:T(8,128)(2,1)S(1)}, bf16[896,896]{1,0:T(8,128)(2,1)}, u32[]{:S(2)}) copy-start(bf16[896,896]{1,0:T(8,128)(2,1)} %copy-done.2) | copy-start | bytes 4816900
where the time goes:
time: 500 us; the launch traced here: 493 us
  waiting for transfers between devices  265 us (53%)
  starting transfers between devices  159 us (32%)
  matrix products  67.4 us (13%)
    ppermute x8, waiting for transfers between devices, from_behind(): return lax.ppermute(block, axis, route)  265 us
    ppermute x8, starting transfers between devices, from_behind(): return lax.ppermute(block, axis, route)  159 us
    dot_general x4, matrix products, cross_weights(): lax.dot_general(left, right, (((1,), (1,)), ((), ())), preferred_element_...  13.2 us
    dot_general x2, matrix products, shards(): lax.dot_general(weight_b, got_img, contract_rows, preferred_element_type=...  11.7 us
    dot_general x2, matrix products, shards(): jnp.dot(weight_a, got_txt, preferred_element_type=jnp.float32)  10.9 us
  transfers between devices with their start and end apart: 8, of which 5 were waited for; matrix products, arithmetic and copies ran while one was open for 12% of the time, Pallas kernels for 0%

commit v1 on v0

v1 whole, which is shorter than its diff:
```python
import functools

import jax
import jax.numpy as jnp
from jax import lax
from jax.experimental import pallas as pl
from jax.experimental.pallas import tpu as pltpu
from jax.sharding import PartitionSpec as P

AXES = ("grp", "dev")
LOG2E = 1.4426950408889634
NT = (((1,), (1,)), ((), ()))
PIECES = (256, 256, 192, 128, 64)
DEVICES = range(128)


def place(device):
    return (device >> 6, (device >> 4) & 3, (device >> 2) & 3, (device >> 1) & 1, device & 1)


def device_at(grp, z, x, half, core):
    return (grp << 6) | ((z & 3) << 4) | ((x & 3) << 2) | (half << 1) | core


def at_y(y, z, x, core):
    return device_at(y & 1, z, x, (y & 3) >> 1, core)


CORE_SWAP = [(d, d ^ 1) for d in DEVICES]
HALF_SWAP = [(d, d ^ 2) for d in DEVICES]


def along_x(device):
    grp, z, x, half, core = place(device)
    return device_at(grp, z, x + (1 if half == 0 else -1), half, core)


ALONG_X = [(d, along_x(d)) for d in DEVICES]


def along_z():
    route = []
    for grp in (0, 1):
        for core in (0, 1):
            for z in range(3):
                route.append((device_at(grp, z, 0, 0, core), device_at(grp, z + 1, 0, 0, core)))
                route.append((device_at(grp, z + 1, 3, 1, core), device_at(grp, z, 3, 1, core)))
    return route


ALONG_Z = along_z()

SEAM = ((2, 3, 1, 0), (1, 0, 2, 3), (3, 3, 0, 0), (0, 0, 3, 3))


def pairs(build):
    route = []
    for y_from, at_from, y_to, at_to in SEAM:
        for core in (0, 1):
            route += build(y_from, at_from, y_to, at_to, core)
    return route


def across_seam(stacked, is_source, in_source_plane):
    quarter = stacked.shape[0] // 4
    sixteenth = quarter // 4
    spread = 0
    for k in (1, 2, 3):
        route = pairs(lambda y, a, v, b, c: [(at_y(y, a, a, c), at_y(y, a, a + k, c))])
        spread = spread + lax.ppermute(stacked[k * quarter : (k + 1) * quarter], AXES, route)
    spread = jnp.where(is_source, stacked[:quarter], spread)
    lanes = 0
    for k in (1, 2, 3):
        route = pairs(lambda y, a, v, b, c: [(at_y(y, a, x, c), at_y(y, a + k, x, c)) for x in range(4)])
        lanes = lanes + lax.ppermute(spread[k * sixteenth : (k + 1) * sixteenth], AXES, route)
    lanes = jnp.where(in_source_plane, spread[:sixteenth], lanes)
    route = pairs(lambda y, a, v, b, c: [(at_y(y, z, x, c), at_y(v, z, x, c)) for z in range(4) for x in range(4)])
    lanes = lax.ppermute(lanes, AXES, route)
    rows = []
    for k in range(4):
        route = pairs(lambda y, a, v, b, c: [(at_y(v, a + k, x, c), at_y(v, b, x, c)) for x in range(4)])
        rows.append(lax.ppermute(lanes, AXES, route))
    rows = jnp.concatenate(rows, axis=0)
    whole = []
    for k in range(4):
        route = pairs(lambda y, a, v, b, c: [(at_y(v, b, a + k, c), at_y(v, b, b, c))])
        whole.append(lax.ppermute(rows, AXES, route))
    return jnp.concatenate(whole, axis=0)


def weights(product, temp, positive):
    exponent = product * (-temp * LOG2E) + 2.0 * LOG2E
    if positive is None:
        return (temp / (1.0 + jnp.exp2(exponent))).astype(jnp.bfloat16)
    exponent = jnp.where(positive, -exponent, exponent)
    return (jnp.where(positive, -temp, temp) / (1.0 + jnp.exp2(exponent))).astype(jnp.bfloat16)


def block_body(count, own, temp, *refs):
    rows, others, rest = refs[0], refs[1 : 1 + count], refs[1 + count :]
    if own:
        partner, out, stacked, weight = rest
    else:
        total, out, stacked, weight = rest

    @pl.when(pl.program_id(0) == 0)
    def _():
        at = 0
        for other in others:
            stacked[at : at + other.shape[0], :] = other[...]
            at += other.shape[0]

    left = rows[...]
    many = stacked.shape[0]
    for at in range(0, many, 256):
        end = min(many, at + 256)
        product = lax.dot_general(left, stacked[at:end, :], NT, preferred_element_type=jnp.float32)
        positive = None
        if own and at < others[0].shape[0]:
            column = at + lax.broadcasted_iota(jnp.int32, product.shape, 1)
            positive = column == partner[...]
        weight[:, at:end] = weights(product, temp, positive)
    grads = jnp.dot(weight[...], stacked[...], preferred_element_type=jnp.float32)
    out[...] = grads if own else grads + total[...]


def accumulate(rows, others, halves, size, temp, partner=None, total=None, block=448):
    height, width = rows.shape
    count = len(others)
    many = count * size
    own = partner is not None
    by_row = lambda i: (i, 0)
    last = partner if own else total
    in_specs = [pl.BlockSpec((block, width), by_row)]
    in_specs += [pl.BlockSpec((size, width), lambda i, half=half: (half, 0)) for half in halves]
    in_specs += [pl.BlockSpec((block, last.shape[1]), by_row)]
    return pl.pallas_call(
        functools.partial(block_body, count, own, temp),
        grid=(height // block,),
        in_specs=in_specs,
        out_specs=pl.BlockSpec((block, width), by_row),
        out_shape=jax.ShapeDtypeStruct((height, width), jnp.float32),
        scratch_shapes=[
            pltpu.VMEM((many, width), jnp.bfloat16),
            pltpu.VMEM((block, many), jnp.bfloat16),
        ],
        input_output_aliases={} if own else {count + 1: 0},
        compiler_params=pltpu.CompilerParams(vmem_limit_bytes=48 * 2**20),
        cost_estimate=pl.CostEstimate(
            flops=4 * height * many * width,
            bytes_accessed=height * width * (6 if own else 10) + many * width * 2,
            transcendentals=2 * height * many,
        ),
    )(rows, *others, last)


def shards(images, texts, image_partner, text_partner):
    height, width = images.shape
    temp = 2.0 * width ** (-0.5)
    index = lax.axis_index(AXES)
    core, half, x, z, grp = index & 1, (index >> 1) & 1, (index >> 2) & 3, (index >> 4) & 3, index >> 6
    first_passes_on = core == half
    carried = ((half == 0) & (x == 0)) | ((half == 1) & (x == 3))
    source_z = jnp.where(half == 0, 0, 3)
    in_source_plane = z == source_z
    is_source = in_source_plane & (x == source_z)

    pieces = []
    at = 0
    for size in PIECES:
        pieces.append(jnp.concatenate([texts[at : at + size], images[at : at + size]], axis=0))
        at += size

    swapped = []
    for j, piece in enumerate(pieces):
        if j >= 2:
            piece, swapped[j - 2] = lax.optimization_barrier((piece, swapped[j - 2]))
        swapped.append(lax.ppermute(piece, AXES, HALF_SWAP))
    partner_images = lax.ppermute(images, AXES, CORE_SWAP)
    partner_texts = lax.ppermute(texts, AXES, CORE_SWAP)

    seam = across_seam(jnp.concatenate(pieces, axis=0), is_source, in_source_plane)

    start = index * height
    grad_images = accumulate(
        images, (texts, partner_texts), (0, 0), height, temp, partner=(image_partner - start)[:, None]
    )
    grad_texts = accumulate(
        texts, (images, partner_images), (0, 0), height, temp, partner=(text_partner - start)[:, None]
    )
    at = 0
    for size, one in zip(PIECES, swapped):
        two = lax.ppermute(one, AXES, ALONG_X)
        two_z = lax.ppermute(two, AXES, ALONG_Z)
        two = jnp.where(carried, two_z + seam[at : at + 2 * size], two)
        at += 2 * size
        three = lax.ppermute(jnp.where(first_passes_on, one, two), AXES, CORE_SWAP)
        others = (one, two, three)
        grad_images = accumulate(images, others, (0, 0, 0), size, temp, total=grad_images)
        grad_texts = accumulate(texts, others, (1, 1, 1), size, temp, total=grad_texts)
    return (grad_images, grad_texts)


def solution(mesh):
    return jax.shard_map(
        shards,
        mesh=mesh,
        in_specs=(P(AXES, None), P(AXES, None), P(AXES), P(AXES)),
        out_specs=(P(AXES, None), P(AXES, None)),
        check_vma=False,
    )
```

time: 500 us -> 410 us (0.82)
  the two profiles are of different devices: /device:TPU:55 before, /device:TPU:1 now
where the time goes in v1:
time: 410 us; the launch traced here: 408 us
  waiting for transfers between devices  208 us (51%)
  Pallas kernels  95.8 us (23%)
  starting transfers between devices  68.6 us (17%)
  other arithmetic  18.1 us (4%)
  local copies, waits for them, and re-layouts  17.4 us (4%)
    pallas_call x12, Pallas kernels, accumulate(): pl.pallas_call(functools.partial(block_body, count, own, temp), grid=(hei...  95.8 us
    ppermute x5, waiting for transfers between devices, shards(): two = lax.ppermute(one, AXES, ALONG_X)  75.5 us
    ppermute x1, waiting for transfers between devices, across_seam(): lanes = lax.ppermute(lanes, AXES, route)  37.6 us
    ppermute x5, waiting for transfers between devices, shards(): two_z = lax.ppermute(two, AXES, ALONG_Z)  36.1 us
    ppermute x3, waiting for transfers between devices, across_seam(): lax.ppermute(stacked[k * quarter:(k + 1) * quarter], AXES, route)  28 us
    ppermute x5, starting transfers between devices, shards(): three = lax.ppermute(jnp.where(first_passes_on, one, two), AXES, CORE_SWAP)  20.5 us
    ppermute x4, waiting for transfers between devices, across_seam(): rows.append(lax.ppermute(lanes, AXES, route))  15.6 us
    ppermute x5, waiting for transfers between devices, shards(): swapped.append(lax.ppermute(piece, AXES, HALF_SWAP))  12.2 us
  transfers between devices with their start and end apart: 37, of which 14 were waited for; matrix products, arithmetic and copies ran while one was open for 7% of the time, Pallas kernels for 21%

profile of v1, /device:TPU:1, one launch (start us, length us, event | category | flops | bytes accessed | tf_op | source)
XLA Modules:
  0.0 408.5 jit_solution(12803319624981124722)
XLA Ops:
  7.6 6.6 %collective-permute-start.6 = (bf16[448,1152]{1,0:T(8,128)(2,1)}, bf16[448,1152]{1,0:T(8,128)(2,1)}, u32[]{:S(2)}, u32[]{:S(2)}) collective-permute-start(bf16[448,1152]{1,0:T(8,128)(2,1)} %get-tuple-element.43), channel_id=1, source_target_pairs={{62,54},{63,55},{64,72},{65,73},{126,118},{127,119},{0,8},{1,9}} | collective-permute-start | bytes 3096584 | tf_op jit(solution)/shard_map/ppermute | solution.py:70
  26.1 3.0 collective-permute-start.18
  29.1 5.9 %collective-permute-done.6 = bf16[448,1152]{1,0:T(8,128)(2,1)} collective-permute-done((bf16[448,1152]{1,0:T(8,128)(2,1)}, bf16[448,1152]{1,0:T(8,128)(2,1)}, u32[]{:S(2)}, u32[]{:S(2)}) %collective-permute-start.6) | collective-permute-done | bytes 1032224 | tf_op jit(solution)/shard_map/ppermute | solution.py:70
  34.9 22.1 %collective-permute-done.5 = bf16[448,1152]{1,0:T(8,128)(2,1)} collective-permute-done((bf16[448,1152]{1,0:T(8,128)(2,1)}, bf16[448,1152]{1,0:T(8,128)(2,1)}, u32[]{:S(2)}, u32[]{:S(2)}) %collective-permute-start.5) | collective-permute-done | bytes 1032224 | tf_op jit(solution)/shard_map/ppermute | solution.py:70
  57.1 2.7 fusion.5
  66.5 12.1 %collective-permute-done.18.refs_1_ = bf16[512,1152]{1,0:T(8,128)(2,1)S(1)} collective-permute-done((bf16[512,1152]{1,0:T(8,128)(2,1)}, bf16[512,1152]{1,0:T(8,128)(2,1)S(1)}, u32[]{:S(2)}, u32[]{:S(2)}) %collective-permute-start.18) | collective-permute-done | bytes 1179680 | tf_op jit(solution)/shard_map/ppermute | solution.py:178
  80.6 2.9 collective-permute-start.19
  84.5 37.6 %collective-permute-done.11 = bf16[112,1152]{1,0:T(8,128)(2,1)} collective-permute-done((bf16[112,1152]{1,0:T(8,128)(2,1)S(1)}, bf16[112,1152]{1,0:T(8,128)(2,1)}, u32[]{:S(2)}, u32[]{:S(2)}) %collective-permute-start.11) | collective-permute-done | bytes 258080 | tf_op jit(solution)/shard_map/ppermute | solution.py:78
  126.1 8.3 %collective-permute-done.12 = bf16[112,1152]{1,0:T(8,128)(2,1)} collective-permute-done((bf16[112,1152]{1,0:T(8,128)(2,1)}, bf16[112,1152]{1,0:T(8,128)(2,1)}, u32[]{:S(2)}, u32[]{:S(2)}) %collective-permute-start.12) | collective-permute-done | bytes 258080 | tf_op jit(solution)/shard_map/ppermute | solution.py:82
  139.4 3.6 collective-permute-done.14
  143.7 3.7 collective-permute-done.15
  156.9 73.6 %collective-permute-done.3 = bf16[128,1152]{1,0:T(8,128)(2,1)} collective-permute-done((bf16[128,1152]{1,0:T(8,128)(2,1)S(1)}, bf16[128,1152]{1,0:T(8,128)(2,1)}, u32[]{:S(2)}, u32[]{:S(2)}) %collective-permute-start.3) | collective-permute-done | bytes 294944 | tf_op jit(solution)/shard_map/ppermute | solution.py:193
  232.8 12.9 %shard_map.65.refs_4_ = f32[896,1152]{1,0:T(8,128)} custom-call(bf16[896,1152]{1,0:T(8,128)(2,1)S(1)} %copy-done, bf16[896,1152]{1,0:T(8,128)(2,1)} %refs_1_.3, bf16[896,1152]{1,0:T(8,128)(2,1)} %collective-permute-done.36.refs_2_, s32[896,1]{1,0:T(8,128)S(1)} %copy-done.2), custom_call_target="tpu_custom_call" | custom-call | flops 7398752256 | bytes 10321920 | tf_op jit(solution)/shard_map/pallas_call | solution.py:137
  254.1 12.7 %shard_map.59.refs_4_ = f32[896,1152]{1,0:T(8,128)} custom-call(bf16[896,1152]{1,0:T(8,128)(2,1)} %refs_1_.3, bf16[896,1152]{1,0:T(8,128)(2,1)S(1)} %copy-done, bf16[896,1152]{1,0:T(8,128)(2,1)} %collective-permute-done.35.refs_2_, s32[896,1]{1,0:T(8,128)S(1)} %copy-done.1), custom_call_target="tpu_custom_call" | custom-call | flops 7398752256 | bytes 10321920 | tf_op jit(solution)/shard_map/pallas_call | solution.py:137
  269.1 2.6 collective-permute-done.25
  271.7 3.2 collective-permute-start.17
  276.3 24.4 %collective-permute-done.28 = bf16[512,1152]{1,0:T(8,128)(2,1)S(1)} collective-permute-done((bf16[512,1152]{1,0:T(8,128)(2,1)}, bf16[512,1152]{1,0:T(8,128)(2,1)S(1)}, u32[]{:S(2)}, u32[]{:S(2)}) %collective-permute-start.28) | collective-permute-done | bytes 1179680 | tf_op jit(solution)/shard_map/ppermute | solution.py:194
  300.7 4.2 %broadcast_select_fusion = (bf16[512,1152]{1,0:T(8,128)(2,1)S(1)}, bf16[512,1152]{1,0:T(8,128)(2,1)S(1)}, bf16[512,1152]{1,0:T(8,128)(2,1)S(1)}, bf16[512,1152]{1,0:T(8,128)(2,1)S(1)}) fusion(bf16[512,1152]{1,0:T(8,128)(2,1)} %collective-permute-done.refs_1_, pred[]{:T(512)S(6)} %eq.28, bf16[512,1152]{1,0:T(8,128)(2,1)} %collective-permute-done.31, ...), kind=kLoop, calls=%fused_computation.10 | loop fusion | flops 9437184 | bytes 14893058 | tf_op jit(solution)/shard_map/jit(_where)/select_n | solution.py:197
  305.0 6.8 %collective-permute-start.34 = (bf16[512,1152]{1,0:T(8,128)(2,1)S(1)}, bf16[512,1152]{1,0:T(8,128)(2,1)S(1)}, u32[]{:S(2)}, u32[]{:S(2)}) collective-permute-start(bf16[512,1152]{1,0:T(8,128)(2,1)S(1)} %get-tuple-element.14), channel_id=1, source_target_pairs={{0,1},{1,0},{2,3},{3,2},{4,5},{5,4},{6,7},{7,6},{8,9},{9,8},{10,11... | collective-permute-start | bytes 3538952 | tf_op jit(solution)/shard_map/ppermute | solution.py:197
  315.3 6.7 %collective-permute-start.22 = (bf16[256,1152]{1,0:T(8,128)(2,1)}, bf16[256,1152]{1,0:T(8,128)(2,1)S(1)}, u32[]{:S(2)}, u32[]{:S(2)}) collective-permute-start(bf16[256,1152]{1,0:T(8,128)(2,1)} %get-tuple-element.20), channel_id=1, source_target_pairs={{0,1},{1,0},{2,3},{3,2},{4,5},{5,4},{6,7},{7,6},{8,9},{9,8},{10,11... | collective-permute-start | bytes 1769480 | tf_op jit(solution)/shard_map/ppermute | solution.py:197
  322.0 10.2 %collective-permute-done.24 = bf16[384,1152]{1,0:T(8,128)(2,1)S(1)} collective-permute-done((bf16[384,1152]{1,0:T(8,128)(2,1)S(1)}, bf16[384,1152]{1,0:T(8,128)(2,1)S(1)}, u32[]{:S(2)}, u32[]{:S(2)}) %collective-permute-start.24) | collective-permute-done | bytes 884768 | tf_op jit(solution)/shard_map/ppermute | solution.py:194
  334.5 3.7 collective-permute-start.26
  338.3 7.4 %shard_map.66.refs_4_ = f32[896,1152]{1,0:T(8,128)} custom-call(bf16[896,1152]{1,0:T(8,128)(2,1)S(1)} %copy-done, bf16[512,1152]{1,0:T(8,128)(2,1)} %collective-permute-done.refs_1_, bf16[512,1152]{1,0:T(8,128)(2,1)S(1)} %get-tuple-element.15.refs_2_, bf16[512,1152]{1,0:T(8,128)(2,1)S(1)} %collective-permute-done.34.refs_3_, ...), custom_call_target="tpu_custom_call", output_to_operand_aliasing={{}: (4, {})} | custom-call | flops 3170893824 | bytes 12091392 | tf_op jit(solution)/shard_map/pallas_call | solution.py:137
  345.7 8.0 %shard_map.60.refs_4_ = f32[896,1152]{1,0:T(8,128)} custom-call(bf16[896,1152]{1,0:T(8,128)(2,1)} %refs_1_.3, bf16[512,1152]{1,0:T(8,128)(2,1)} %collective-permute-done.refs_1_, bf16[512,1152]{1,0:T(8,128)(2,1)S(1)} %get-tuple-element.15.refs_2_, bf16[512,1152]{1,0:T(8,128)(2,1)S(1)} %collective-permute-done.34.refs_3_, ...), custom_call_target="tpu_custom_call", output_to_operand_aliasing={{}: (4, {})} | custom-call | flops 3170893824 | bytes 12091392 | tf_op jit(solution)/shard_map/pallas_call | solution.py:137
  353.7 7.3 %shard_map.67.refs_4_ = f32[896,1152]{1,0:T(8,128)} custom-call(bf16[896,1152]{1,0:T(8,128)(2,1)S(1)} %copy-done, bf16[512,1152]{1,0:T(8,128)(2,1)S(1)} %collective-permute-done.18.refs_1_, bf16[512,1152]{1,0:T(8,128)(2,1)S(1)} %get-tuple-element.39.refs_2_, bf16[512,1152]{1,0:T(8,128)(2,1)S(1)} %collective-permute-done.30.refs_3_, ...), custom_call_target="tpu_custom_call", output_to_operand_aliasing={{}: (4, {})} | custom-call | flops 3170893824 | bytes 12091392 | tf_op jit(solution)/shard_map/pallas_call | solution.py:137
  361.0 7.5 %shard_map.68.refs_4_ = f32[896,1152]{1,0:T(8,128)} custom-call(bf16[896,1152]{1,0:T(8,128)(2,1)S(1)} %copy-done, bf16[384,1152]{1,0:T(8,128)(2,1)} %collective-permute-done.1.refs_1_, bf16[384,1152]{1,0:T(8,128)(2,1)S(1)} %get-tuple-element.19.refs_2_, bf16[384,1152]{1,0:T(8,128)(2,1)S(1)} %collective-permute-done.26.refs_3_, ...), custom_call_target="tpu_custom_call", output_to_operand_aliasing={{}: (4, {})} | custom-call | flops 2378170368 | bytes 11649024 | tf_op jit(solution)/shard_map/pallas_call | solution.py:137
  368.5 7.6 %shard_map.61.refs_4_ = f32[896,1152]{1,0:T(8,128)} custom-call(bf16[896,1152]{1,0:T(8,128)(2,1)} %refs_1_.3, bf16[512,1152]{1,0:T(8,128)(2,1)S(1)} %collective-permute-done.18.refs_1_, bf16[512,1152]{1,0:T(8,128)(2,1)S(1)} %get-tuple-element.39.refs_2_, bf16[512,1152]{1,0:T(8,128)(2,1)S(1)} %collective-permute-done.30.refs_3_, ...), custom_call_target="tpu_custom_call", output_to_operand_aliasing={{}: (4, {})} | custom-call | flops 3170893824 | bytes 12091392 | tf_op jit(solution)/shard_map/pallas_call | solution.py:137
  376.1 8.1 %shard_map.62.refs_4_ = f32[896,1152]{1,0:T(8,128)} custom-call(bf16[896,1152]{1,0:T(8,128)(2,1)} %refs_1_.3, bf16[384,1152]{1,0:T(8,128)(2,1)} %collective-permute-done.1.refs_1_, bf16[384,1152]{1,0:T(8,128)(2,1)S(1)} %get-tuple-element.19.refs_2_, bf16[384,1152]{1,0:T(8,128)(2,1)S(1)} %collective-permute-done.26.refs_3_, ...), custom_call_target="tpu_custom_call", output_to_operand_aliasing={{}: (4, {})} | custom-call | flops 2378170368 | bytes 11649024 | tf_op jit(solution)/shard_map/pallas_call | solution.py:137
  384.2 5.9 %shard_map.69.refs_4_ = f32[896,1152]{1,0:T(8,128)} custom-call(bf16[896,1152]{1,0:T(8,128)(2,1)S(1)} %copy-done, bf16[256,1152]{1,0:T(8,128)(2,1)} %collective-permute-done.19.refs_1_, bf16[256,1152]{1,0:T(8,128)(2,1)S(1)} %get-tuple-element.21.refs_2_, bf16[256,1152]{1,0:T(8,128)(2,1)S(1)} %collective-permute-done.22.refs_3_, ...), custom_call_target="tpu_custom_call", output_to_operand_aliasing={{}: (4, {})} | custom-call | flops 1585446912 | bytes 11206656 | tf_op jit(solution)/shard_map/pallas_call | solution.py:137
  390.1 6.5 %shard_map.63.refs_4_ = f32[896,1152]{1,0:T(8,128)} custom-call(bf16[896,1152]{1,0:T(8,128)(2,1)} %refs_1_.3, bf16[256,1152]{1,0:T(8,128)(2,1)} %collective-permute-done.19.refs_1_, bf16[256,1152]{1,0:T(8,128)(2,1)S(1)} %get-tuple-element.21.refs_2_, bf16[256,1152]{1,0:T(8,128)(2,1)S(1)} %collective-permute-done.22.refs_3_, ...), custom_call_target="tpu_custom_call", output_to_operand_aliasing={{}: (4, {})} | custom-call | flops 1585446912 | bytes 11206656 | tf_op jit(solution)/shard_map/pallas_call | solution.py:137
  396.6 5.8 %shard_map.70 = f32[896,1152]{1,0:T(8,128)} custom-call(bf16[896,1152]{1,0:T(8,128)(2,1)S(1)} %copy-done, bf16[128,1152]{1,0:T(8,128)(2,1)S(1)} %collective-permute-done.2.refs_1_, bf16[128,1152]{1,0:T(8,128)(2,1)S(1)} %get-tuple-element.23.refs_2_, bf16[128,1152]{1,0:T(8,128)(2,1)S(1)} %collective-permute-done.17.refs_3_, ...), custom_call_target="tpu_custom_call", output_to_operand_aliasing={{}: (4, {})} | custom-call | flops 792723456 | bytes 10764288 | tf_op jit(solution)/shard_map/pallas_call | solution.py:137
  402.4 6.1 %shard_map.64 = f32[896,1152]{1,0:T(8,128)} custom-call(bf16[896,1152]{1,0:T(8,128)(2,1)} %refs_1_.3, bf16[128,1152]{1,0:T(8,128)(2,1)S(1)} %collective-permute-done.2.refs_1_, bf16[128,1152]{1,0:T(8,128)(2,1)S(1)} %get-tuple-element.23.refs_2_, bf16[128,1152]{1,0:T(8,128)(2,1)S(1)} %collective-permute-done.17.refs_3_, ...), custom_call_target="tpu_custom_call", output_to_operand_aliasing={{}: (4, {})} | custom-call | flops 792723456 | bytes 10764288 | tf_op jit(solution)/shard_map/pallas_call | solution.py:137
  (112 shorter events, 67.8 us)
Async XLA Ops:
  7.6 27.4 %collective-permute-start.6 = (bf16[448,1152]{1,0:T(8,128)(2,1)}, bf16[448,1152]{1,0:T(8,128)(2,1)}, u32[]{:S(2)}, u32[]{:S(2)}) collective-permute-start(bf16[448,1152]{1,0:T(8,128)(2,1)} %get-tuple-element.43), channel_id=1, source_target_pairs={{62,54},{63,55},{64,72},{65,73},{126,118},{127,119},{0,8},{1,9}} | collective-permute-start | bytes 3096584 | tf_op jit(solution)/shard_map/ppermute | solution.py:70
  14.2 42.9 %collective-permute-start.5 = (bf16[448,1152]{1,0:T(8,128)(2,1)}, bf16[448,1152]{1,0:T(8,128)(2,1)}, u32[]{:S(2)}, u32[]{:S(2)}) collective-permute-start(bf16[448,1152]{1,0:T(8,128)(2,1)} %get-tuple-element.44), channel_id=1, source_target_pairs={{62,50},{63,51},{64,68},{65,69},{126,114},{127,115},{0,4},{1,5}} | collective-permute-start | bytes 3096584 | tf_op jit(solution)/shard_map/ppermute | solution.py:70
  21.6 35.4 %collective-permute-start.7 = (bf16[448,1152]{1,0:T(8,128)(2,1)}, bf16[448,1152]{1,0:T(8,128)(2,1)}, u32[]{:S(2)}, u32[]{:S(2)}) collective-permute-start(bf16[448,1152]{1,0:T(8,128)(2,1)} %slice.100), channel_id=1, source_target_pairs={{62,58},{63,59},{64,76},{65,77},{126,122},{127,123},{0,12},{1,13}} | collective-permute-start | bytes 3096584 | tf_op jit(solution)/shard_map/ppermute | solution.py:70
  25.0 39.9 %collective-permute-start = (bf16[512,1152]{1,0:T(8,128)(2,1)}, bf16[512,1152]{1,0:T(8,128)(2,1)}, u32[]{:S(2)}, u32[]{:S(2)}) collective-permute-start(bf16[512,1152]{1,0:T(8,128)(2,1)} %pad_maximum_fusion), channel_id=1, source_target_pairs={{0,2},{1,3},{2,0},{3,1},{4,6},{5,7},{6,4},{7,5},{8,10},{9,11},{10,... | collective-permute-start | bytes 3538952 | tf_op jit(solution)/shard_map/ppermute | solution.py:178
  26.1 52.4 %collective-permute-start.18 = (bf16[512,1152]{1,0:T(8,128)(2,1)}, bf16[512,1152]{1,0:T(8,128)(2,1)S(1)}, u32[]{:S(2)}, u32[]{:S(2)}) collective-permute-start(bf16[512,1152]{1,0:T(8,128)(2,1)} %pad_maximum_fusion.3), channel_id=1, source_target_pairs={{0,2},{1,3},{2,0},{3,1},{4,6},{5,7},{6,4},{7,5},{8,10},{9,11},{10,... | collective-permute-start | bytes 3538952 | tf_op jit(solution)/shard_map/ppermute | solution.py:178
  59.8 20.6 %collective-permute-start.9 = (bf16[112,1152]{1,0:T(8,128)(2,1)S(1)}, bf16[112,1152]{1,0:T(8,128)(2,1)S(1)}, u32[]{:S(2)}, u32[]{:S(2)}) collective-permute-start(bf16[112,1152]{1,0:T(8,128)(2,1)S(1)} %get-tuple-element.40), channel_id=1, source_target_pairs={{50,18},{54,22},{58,26},{62,30},{51,19},{55,23},{59,27},{63,31},{6... | collective-permute-start | bytes 774152 | tf_op jit(solution)/shard_map/ppermute | solution.py:75
  61.3 19.3 %collective-permute-start.10 = (bf16[112,1152]{1,0:T(8,128)(2,1)S(1)}, bf16[112,1152]{1,0:T(8,128)(2,1)S(1)}, u32[]{:S(2)}, u32[]{:S(2)}) collective-permute-start(bf16[112,1152]{1,0:T(8,128)(2,1)S(1)} %get-tuple-element.41), channel_id=1, source_target_pairs={{50,34},{54,38},{58,42},{62,46},{51,35},{55,39},{59,43},{63,47},{6... | collective-permute-start | bytes 774152 | tf_op jit(solution)/shard_map/ppermute | solution.py:75
  62.6 20.9 %collective-permute-start.8 = (bf16[112,1152]{1,0:T(8,128)(2,1)S(1)}, bf16[112,1152]{1,0:T(8,128)(2,1)S(1)}, u32[]{:S(2)}, u32[]{:S(2)}) collective-permute-start(bf16[112,1152]{1,0:T(8,128)(2,1)S(1)} %get-tuple-element.42), channel_id=1, source_target_pairs={{50,2},{54,6},{58,10},{62,14},{51,3},{55,7},{59,11},{63,15},{64,80... | collective-permute-start | bytes 774152 | tf_op jit(solution)/shard_map/ppermute | solution.py:75
  64.9 83.2 %collective-permute-start.36 = (bf16[896,1152]{1,0:T(8,128)(2,1)}, bf16[896,1152]{1,0:T(8,128)(2,1)}, u32[]{:S(2)}, u32[]{:S(2)}) collective-permute-start(bf16[896,1152]{1,0:T(8,128)(2,1)} %refs_1_.3), channel_id=1, source_target_pairs={{0,1},{1,0},{2,3},{3,2},{4,5},{5,4},{6,7},{7,6},{8,9},{9,8},{10,11... | collective-permute-start | bytes 6193160 | tf_op jit(solution)/shard_map/ppermute | solution.py:179
  78.5 70.8 %collective-permute-start.35 = (bf16[896,1152]{1,0:T(8,128)(2,1)S(1)}, bf16[896,1152]{1,0:T(8,128)(2,1)}, u32[]{:S(2)}, u32[]{:S(2)}) collective-permute-start(bf16[896,1152]{1,0:T(8,128)(2,1)S(1)} %copy-done), channel_id=1, source_target_pairs={{0,1},{1,0},{2,3},{3,2},{4,5},{5,4},{6,7},{7,6},{8,9},{9,8},{10,11... | collective-permute-start | bytes 6193160 | tf_op jit(solution)/shard_map/ppermute | solution.py:180
  80.5 56.9 %collective-permute-start.1 = (bf16[384,1152]{1,0:T(8,128)(2,1)}, bf16[384,1152]{1,0:T(8,128)(2,1)}, u32[]{:S(2)}, u32[]{:S(2)}) collective-permute-start(bf16[384,1152]{1,0:T(8,128)(2,1)} %pad_maximum_fusion.9), channel_id=1, source_target_pairs={{0,2},{1,3},{2,0},{3,1},{4,6},{5,7},{6,4},{7,5},{8,10},{9,11},{10,... | collective-permute-start | bytes 2654216 | tf_op jit(solution)/shard_map/ppermute | solution.py:178
  80.6 43.1 %collective-permute-start.19 = (bf16[256,1152]{1,0:T(8,128)(2,1)S(1)}, bf16[256,1152]{1,0:T(8,128)(2,1)}, u32[]{:S(2)}, u32[]{:S(2)}) collective-permute-start(bf16[256,1152]{1,0:T(8,128)(2,1)S(1)} %pad_maximum_fusion.10), channel_id=1, source_target_pairs={{0,2},{1,3},{2,0},{3,1},{4,6},{5,7},{6,4},{7,5},{8,10},{9,11},{10,... | collective-permute-start | bytes 1769480 | tf_op jit(solution)/shard_map/ppermute | solution.py:178
  83.6 38.5 %collective-permute-start.11 = (bf16[112,1152]{1,0:T(8,128)(2,1)S(1)}, bf16[112,1152]{1,0:T(8,128)(2,1)}, u32[]{:S(2)}, u32[]{:S(2)}) collective-permute-start(bf16[112,1152]{1,0:T(8,128)(2,1)S(1)} %slice_select_fusion), channel_id=1, source_target_pairs={{2,64},{6,68},{10,72},{14,76},{18,80},{22,84},{26,88},{30,92},{34,... | collective-permute-start | bytes 774152 | tf_op jit(solution)/shard_map/ppermute | solution.py:78
  126.0 28.6 %collective-permute-start.31 = (bf16[512,1152]{1,0:T(8,128)(2,1)}, bf16[512,1152]{1,0:T(8,128)(2,1)}, u32[]{:S(2)}, u32[]{:S(2)}) collective-permute-start(bf16[512,1152]{1,0:T(8,128)(2,1)} %collective-permute-done.refs_1_), channel_id=1, source_target_pairs={{0,4},{1,5},{2,14},{3,15},{4,8},{5,9},{6,2},{7,3},{8,12},{9,13},{1... | collective-permute-start | bytes 3538952 | tf_op jit(solution)/shard_map/ppermute | solution.py:193
  147.3 100.3 %collective-permute-start.27 = (bf16[512,1152]{1,0:T(8,128)(2,1)S(1)}, bf16[512,1152]{1,0:T(8,128)(2,1)}, u32[]{:S(2)}, u32[]{:S(2)}) collective-permute-start(bf16[512,1152]{1,0:T(8,128)(2,1)S(1)} %collective-permute-done.18.refs_1_), channel_id=1, source_target_pairs={{0,4},{1,5},{2,14},{3,15},{4,8},{5,9},{6,2},{7,3},{8,12},{9,13},{1... | collective-permute-start | bytes 3538952 | tf_op jit(solution)/shard_map/ppermute | solution.py:193
  148.1 100.8 %collective-permute-start.33 = (bf16[448,1152]{1,0:T(8,128)(2,1)}, bf16[448,1152]{1,0:T(8,128)(2,1)}, u32[]{:S(2)}, u32[]{:S(2)}) collective-permute-start(bf16[448,1152]{1,0:T(8,128)(2,1)} %constant_dynamic-update-slice_fusion.5), channel_id=1, source_target_pairs={{76,64},{77,65},{50,62},{51,63},{12,0},{13,1},{114,126},{115,127}} | collective-permute-start | bytes 3096584 | tf_op jit(solution)/shard_map/ppermute | solution.py:87
  149.4 101.8 %collective-permute-start.16 = (bf16[448,1152]{1,0:T(8,128)(2,1)}, bf16[448,1152]{1,0:T(8,128)(2,1)}, u32[]{:S(2)}, u32[]{:S(2)}) collective-permute-start(bf16[448,1152]{1,0:T(8,128)(2,1)} %constant_dynamic-update-slice_fusion.5), channel_id=1, source_target_pairs={{72,64},{73,65},{62,62},{63,63},{8,0},{9,1},{126,126},{127,127}} | collective-permute-start | bytes 3096584 | tf_op jit(solution)/shard_map/ppermute | solution.py:87
  150.8 79.7 %collective-permute-start.3 = (bf16[128,1152]{1,0:T(8,128)(2,1)S(1)}, bf16[128,1152]{1,0:T(8,128)(2,1)}, u32[]{:S(2)}, u32[]{:S(2)}) collective-permute-start(bf16[128,1152]{1,0:T(8,128)(2,1)S(1)} %collective-permute-done.2.refs_1_), channel_id=1, source_target_pairs={{0,4},{1,5},{2,14},{3,15},{4,8},{5,9},{6,2},{7,3},{8,12},{9,13},{1... | collective-permute-start | bytes 884744 | tf_op jit(solution)/shard_map/ppermute | solution.py:193
  154.6 91.1 %collective-permute-start.20 = (bf16[256,1152]{1,0:T(8,128)(2,1)}, bf16[256,1152]{1,0:T(8,128)(2,1)S(1)}, u32[]{:S(2)}, u32[]{:S(2)}) collective-permute-start(bf16[256,1152]{1,0:T(8,128)(2,1)} %collective-permute-done.19.refs_1_), channel_id=1, source_target_pairs={{0,4},{1,5},{2,14},{3,15},{4,8},{5,9},{6,2},{7,3},{8,12},{9,13},{1... | collective-permute-start | bytes 1769480 | tf_op jit(solution)/shard_map/ppermute | solution.py:193
  230.5 22.2 %collective-permute-start.4 = (bf16[128,1152]{1,0:T(8,128)(2,1)}, bf16[128,1152]{1,0:T(8,128)(2,1)S(1)}, u32[]{:S(2)}, u32[]{:S(2)}) collective-permute-start(bf16[128,1152]{1,0:T(8,128)(2,1)} %collective-permute-done.3), channel_id=1, source_target_pairs={{0,16},{30,14},{16,32},{46,30},{32,48},{62,46},{1,17},{31,15},{17,... | collective-permute-start | bytes 884744 | tf_op jit(solution)/shard_map/ppermute | solution.py:194
  245.7 22.0 %collective-permute-start.29 = (bf16[448,1152]{1,0:T(8,128)(2,1)}, bf16[448,1152]{1,0:T(8,128)(2,1)S(1)}, u32[]{:S(2)}, u32[]{:S(2)}) collective-permute-start(bf16[448,1152]{1,0:T(8,128)(2,1)} %constant_dynamic-update-slice_fusion.5), channel_id=1, source_target_pairs={{64,64},{65,65},{54,62},{55,63},{0,0},{1,1},{118,126},{119,127}} | collective-permute-start | bytes 3096584 | tf_op jit(solution)/shard_map/ppermute | solution.py:87
  247.6 24.1 %collective-permute-start.25 = (bf16[448,1152]{1,0:T(8,128)(2,1)}, bf16[448,1152]{1,0:T(8,128)(2,1)S(1)}, u32[]{:S(2)}, u32[]{:S(2)}) collective-permute-start(bf16[448,1152]{1,0:T(8,128)(2,1)} %constant_dynamic-update-slice_fusion.5), channel_id=1, source_target_pairs={{68,64},{69,65},{58,62},{59,63},{4,0},{5,1},{122,126},{123,127}} | collective-permute-start | bytes 3096584 | tf_op jit(solution)/shard_map/ppermute | solution.py:87
  248.9 26.0 %collective-permute-start.23 = (bf16[384,1152]{1,0:T(8,128)(2,1)}, bf16[384,1152]{1,0:T(8,128)(2,1)S(1)}, u32[]{:S(2)}, u32[]{:S(2)}) collective-permute-start(bf16[384,1152]{1,0:T(8,128)(2,1)} %collective-permute-done.1.refs_1_), channel_id=1, source_target_pairs={{0,4},{1,5},{2,14},{3,15},{4,8},{5,9},{6,2},{7,3},{8,12},{9,13},{1... | collective-permute-start | bytes 2654216 | tf_op jit(solution)/shard_map/ppermute | solution.py:193
  251.1 25.2 %collective-permute-start.32 = (bf16[512,1152]{1,0:T(8,128)(2,1)}, bf16[512,1152]{1,0:T(8,128)(2,1)S(1)}, u32[]{:S(2)}, u32[]{:S(2)}) collective-permute-start(bf16[512,1152]{1,0:T(8,128)(2,1)} %collective-permute-done.31), channel_id=1, source_target_pairs={{0,16},{30,14},{16,32},{46,30},{32,48},{62,46},{1,17},{31,15},{17,... | collective-permute-start | bytes 3538952 | tf_op jit(solution)/shard_map/ppermute | solution.py:194
  252.7 48.0 %collective-permute-start.28 = (bf16[512,1152]{1,0:T(8,128)(2,1)}, bf16[512,1152]{1,0:T(8,128)(2,1)S(1)}, u32[]{:S(2)}, u32[]{:S(2)}) collective-permute-start(bf16[512,1152]{1,0:T(8,128)(2,1)} %collective-permute-done.27), channel_id=1, source_target_pairs={{0,16},{30,14},{16,32},{46,30},{32,48},{62,46},{1,17},{31,15},{17,... | collective-permute-start | bytes 3538952 | tf_op jit(solution)/shard_map/ppermute | solution.py:194
  267.8 45.5 %collective-permute-start.21 = (bf16[256,1152]{1,0:T(8,128)(2,1)S(1)}, bf16[256,1152]{1,0:T(8,128)(2,1)S(1)}, u32[]{:S(2)}, u32[]{:S(2)}) collective-permute-start(bf16[256,1152]{1,0:T(8,128)(2,1)S(1)} %collective-permute-done.20), channel_id=1, source_target_pairs={{0,16},{30,14},{16,32},{46,30},{32,48},{62,46},{1,17},{31,15},{17,... | collective-permute-start | bytes 1769480 | tf_op jit(solution)/shard_map/ppermute | solution.py:194
  271.7 124.9 %collective-permute-start.17 = (bf16[128,1152]{1,0:T(8,128)(2,1)S(1)}, bf16[128,1152]{1,0:T(8,128)(2,1)S(1)}, u32[]{:S(2)}, u32[]{:S(2)}) collective-permute-start(bf16[128,1152]{1,0:T(8,128)(2,1)S(1)} %get-tuple-element.22), channel_id=1, source_target_pairs={{0,1},{1,0},{2,3},{3,2},{4,5},{5,4},{6,7},{7,6},{8,9},{9,8},{10,11... | collective-permute-start | bytes 884744 | tf_op jit(solution)/shard_map/ppermute | solution.py:197
  274.9 57.3 %collective-permute-start.24 = (bf16[384,1152]{1,0:T(8,128)(2,1)S(1)}, bf16[384,1152]{1,0:T(8,128)(2,1)S(1)}, u32[]{:S(2)}, u32[]{:S(2)}) collective-permute-start(bf16[384,1152]{1,0:T(8,128)(2,1)S(1)} %collective-permute-done.23), channel_id=1, source_target_pairs={{0,16},{30,14},{16,32},{46,30},{32,48},{62,46},{1,17},{31,15},{17,... | collective-permute-start | bytes 2654216 | tf_op jit(solution)/shard_map/ppermute | solution.py:194
  305.0 33.3 %collective-permute-start.34 = (bf16[512,1152]{1,0:T(8,128)(2,1)S(1)}, bf16[512,1152]{1,0:T(8,128)(2,1)S(1)}, u32[]{:S(2)}, u32[]{:S(2)}) collective-permute-start(bf16[512,1152]{1,0:T(8,128)(2,1)S(1)} %get-tuple-element.14), channel_id=1, source_target_pairs={{0,1},{1,0},{2,3},{3,2},{4,5},{5,4},{6,7},{7,6},{8,9},{9,8},{10,11... | collective-permute-start | bytes 3538952 | tf_op jit(solution)/shard_map/ppermute | solution.py:197
  315.3 68.9 %collective-permute-start.22 = (bf16[256,1152]{1,0:T(8,128)(2,1)}, bf16[256,1152]{1,0:T(8,128)(2,1)S(1)}, u32[]{:S(2)}, u32[]{:S(2)}) collective-permute-start(bf16[256,1152]{1,0:T(8,128)(2,1)} %get-tuple-element.20), channel_id=1, source_target_pairs={{0,1},{1,0},{2,3},{3,2},{4,5},{5,4},{6,7},{7,6},{8,9},{9,8},{10,11... | collective-permute-start | bytes 1769480 | tf_op jit(solution)/shard_map/ppermute | solution.py:197
  322.0 31.7 %collective-permute-start.30 = (bf16[512,1152]{1,0:T(8,128)(2,1)S(1)}, bf16[512,1152]{1,0:T(8,128)(2,1)S(1)}, u32[]{:S(2)}, u32[]{:S(2)}) collective-permute-start(bf16[512,1152]{1,0:T(8,128)(2,1)S(1)} %get-tuple-element.38), channel_id=1, source_target_pairs={{0,1},{1,0},{2,3},{3,2},{4,5},{5,4},{6,7},{7,6},{8,9},{9,8},{10,11... | collective-permute-start | bytes 3538952 | tf_op jit(solution)/shard_map/ppermute | solution.py:197
  334.5 26.5 %collective-permute-start.26 = (bf16[384,1152]{1,0:T(8,128)(2,1)}, bf16[384,1152]{1,0:T(8,128)(2,1)S(1)}, u32[]{:S(2)}, u32[]{:S(2)}) collective-permute-start(bf16[384,1152]{1,0:T(8,128)(2,1)} %get-tuple-element.18), channel_id=1, source_target_pairs={{0,1},{1,0},{2,3},{3,2},{4,5},{5,4},{6,7},{7,6},{8,9},{9,8},{10,11... | collective-permute-start | bytes 2654216 | tf_op jit(solution)/shard_map/ppermute | solution.py:197
  (19 other events, 424.3 us)
